TPU v7x, 128 devices: a whole 4x4x4 slice. The times are simulated.
128 devices in a mesh: lon: 64 (over y, z_lo, x, core), lat: 2 (over z_hi).
Axes of the slice: x: 4, y: 4, z: 4 (z_hi: 2, z_lo: 2; z = z_hi * 2 + z_lo), core: 2. Of those that a mesh axis runs over, the one named last changes fastest.
Arguments:
- surface: float32 [64, 655360], P('lon'), may hold values from -6 to 6
- fidelity: float32 [64, 655360], P('lon'), may hold values from 0.5 to 4
- smoothing: float32 [64, 655360], P('lat', 'lon'), may hold values from 0.1 to 1
Outputs:
- heights: float32 [64, 655360], P('lat', 'lon')
- dual_x: float32 [64, 655360], P('lat', 'lon')
- dual_y: float32 [64, 655360], P('lat', 'lon')
- gap: float32 [3], replicated
All inputs are finite; a program needn't handle non-finite values.
Results may differ from a plain program's by a relative error of at most 0.0001.
Values sent between devices are 32-bit elements; how exact they have to be, the bound alone decides.
A program may use at most 128 MiB of HBM per device.

v0:
```python
import jax
import jax.numpy as jnp
from jax import lax
from jax.sharding import PartitionSpec as P

ITERS = 3


primal_step = 0.35
dual_step = 0.35


def shifted(value, axis, steps):
    count = lax.axis_size(axis)
    pairs = [(source, (source + steps) % count) for source in range(count)]
    return lax.ppermute(value, axis, pairs)


def passed_along(block, axis, distance):
    devices = range(lax.axis_size(axis))
    route = [(i - distance, i) for i in devices if i - distance in devices]
    return lax.ppermute(block, axis, route)


def project(dual_x, dual_y, grad_x, grad_y, weight):
    cand_x = dual_x + dual_step * grad_x
    cand_y = dual_y + dual_step * grad_y
    shrink = jnp.maximum(1.0, jnp.sqrt(cand_x * cand_x + cand_y * cand_y) / weight)
    return (cand_x / shrink, cand_y / shrink)


def advance(heights, surface, fidelity, smoothing, diverge, slope_x, slope_y):
    misfit = heights - surface
    terms = (
        0.5 * fidelity * misfit * misfit
        + smoothing * jnp.sqrt(slope_x * slope_x + slope_y * slope_y)
        + surface * diverge
        + 0.5 * diverge * diverge / fidelity
    )
    updated = (heights + primal_step * diverge + primal_step * fidelity * surface) / (
        1.0 + primal_step * fidelity
    )
    return (updated, jnp.sum(terms))


def on_device(surface, fidelity, smoothing):
    whole_surface, whole_fidelity = (
        lax.all_to_all(surface, "lon", split_axis=1, concat_axis=0, tiled=True),
        lax.all_to_all(fidelity, "lon", split_axis=1, concat_axis=0, tiled=True),
    )
    rows, cols = smoothing.shape
    lat_pos = lax.axis_index("lat")
    surface = lax.dynamic_slice_in_dim(whole_surface, lat_pos * rows, rows, 0)
    fidelity = lax.dynamic_slice_in_dim(whole_fidelity, lat_pos * rows, rows, 0)
    total_rows = rows * lax.axis_size("lat")
    cells = rows * cols * lax.axis_size("lat") * lax.axis_size("lon")
    heights = surface
    lead = surface
    gaps = []
    global_row = lat_pos * rows + lax.broadcasted_iota(jnp.int32, (rows, 1), 0)
    keep_y = global_row < total_rows - 1
    dual_x = jnp.zeros_like(surface)
    dual_y = jnp.zeros_like(surface)
    for step in range(ITERS):
        stacked = jnp.stack([lead, heights])
        east = shifted(stacked[:, :, :1], "lon", -1)
        south = passed_along(stacked[:, :1, :], "lat", -1)
        grad_x = jnp.concatenate([stacked[:, :, 1:], east], axis=2) - stacked
        grad_y = jnp.where(
            keep_y, jnp.concatenate([stacked[:, 1:, :], south], axis=1) - stacked, 0.0
        )
        dual_x, dual_y = project(dual_x, dual_y, grad_x[0], grad_y[0], smoothing)
        west = shifted(dual_x[:, -1:], "lon", 1)
        north = passed_along(dual_y[-1:, :], "lat", 1)
        diverge = (
            dual_x
            - jnp.concatenate([west, dual_x[:, :-1]], axis=1)
            + dual_y
            - jnp.concatenate([north, dual_y[:-1]], axis=0)
        )
        slope_x = grad_x[1]
        slope_y = grad_y[1]
        updated, local_gap = advance(
            heights, surface, fidelity, smoothing, diverge, slope_x, slope_y
        )
        gaps.append(lax.psum(local_gap, ("lon", "lat")) / cells)
        lead = 2.0 * updated - heights
        heights = updated
    gap = jnp.stack(gaps)
    return (heights, dual_x, dual_y, gap)


def solution(mesh):
    in_specs = (P("lon", None), P("lon", None), P("lat", "lon"))
    out_specs = (P("lat", "lon"), P("lat", "lon"), P("lat", "lon"), P())
    return jax.shard_map(
        on_device, mesh=mesh, in_specs=in_specs, out_specs=out_specs, check_vma=False
    )
```

profile of v0, /device:TPU:1, one launch (start us, length us, event | category | flops | bytes accessed | tf_op | source)
XLA Modules:
  0.0 216.1 jit_solution(16830832024072321621)
XLA Ops:
  0.6 10.4 %all-to-all-start = ((f32[1,64,10240]{2,0,1:T(1,128)}), f32[1,64,10240]{2,0,1:T(1,128)S(1)}, u32[]{:S(2)}, u32[]{:S(2)}) async-start(f32[1,64,10240]{2,0,1:T(1,128)} %bitcast.161), calls=%async_computation | async-start | bytes 5242880 | tf_op jit(solution)/shard_map/all_to_all | solution.py:48
  11.0 35.0 %all-to-all-done = f32[1,64,10240]{2,0,1:T(1,128)S(1)} async-done(((f32[1,64,10240]{2,0,1:T(1,128)}), f32[1,64,10240]{2,0,1:T(1,128)S(1)}, u32[]{:S(2)}, u32[]{:S(2)}) %all-to-all-start) | async-done | bytes 2621472 | tf_op jit(solution)/shard_map/all_to_all | solution.py:48
  46.0 1.6 copy-done.10
  47.5 5.1 %all-to-all-start.1 = ((f32[1,64,10240]{2,0,1:T(1,128)}), f32[1,64,10240]{2,0,1:T(1,128)}, u32[]{:S(2)}, u32[]{:S(2)}) async-start(f32[1,64,10240]{2,0,1:T(1,128)} %bitcast.162), calls=%async_computation.1 | async-start | bytes 5242880 | tf_op jit(solution)/shard_map/all_to_all | solution.py:49
  52.7 1.4 constant_dynamic-slice_fusion.1
  55.4 1.3 collective-permute-start.1
  57.7 25.6 %collective-permute-done = f32[2,32,1]{2,1,0:T(8,128)S(1)} collective-permute-done((f32[2,32,1]{2,1,0:T(8,128)S(1)}, f32[2,32,1]{2,1,0:T(8,128)S(1)}, u32[]{:S(2)}, u32[]{:S(2)}) %collective-permute-start) | collective-permute-done | bytes 288 | tf_op jit(solution)/shard_map/ppermute | solution.py:16
  83.3 2.4 %collective-permute-done.1 = f32[2,1,10240]{2,1,0:T(1,128)S(1)} collective-permute-done((f32[2,1,10240]{2,1,0:T(1,128)S(1)}, f32[2,1,10240]{2,1,0:T(1,128)S(1)}, u32[]{:S(2)}, u32[]{:S(2)}) %collective-permute-start.1) | collective-permute-done | bytes 81952 | tf_op jit(solution)/shard_map/ppermute | solution.py:22
  86.4 0.8 fusion.58
  87.1 0.7 copy-done.6
  88.6 1.1 copy-done
  89.7 2.0 collective-permute-start.2
  91.8 1.3 collective-permute-start.3
  93.1 1.5 constant_dynamic-slice_fusion
  94.8 2.7 %fusion.52 = (f32[1,32,10240]{2,1,0:T(8,128)S(1)}, f32[32,10240]{1,0:T(8,128)S(1)}, f32[32,10240]{1,0:T(8,128)}) fusion(f32[1,32,10240]{2,0,1:T(1,128)S(1)} %constant_dynamic-slice_fusion.1, f32[1,32,10240]{2,0,1:T(1,128)S(1)} %constant_dynamic-slice_fusion, f32[31,10240]{1,0:T(8,128)S(1)} %bitcast.155, f32[1,10240]{1,0:T(1,128)S(1)} %collective-permute-done.3, ...), kind=kLoop, calls=%fused_computation.108 | loop fusion | flops 4587520 | bytes 11796480 | tf_op jit(solution)/shard_map/stack | solution.py:65
  97.6 0.7 fusion.2
  98.3 3.0 %collective-permute-start.4 = (f32[2,32,1]{2,1,0:T(8,128)S(1)}, f32[2,32,1]{2,1,0:T(8,128)S(1)}, u32[]{:S(2)}, u32[]{:S(2)}) collective-permute-start(f32[2,32,1]{2,1,0:T(8,128)S(1)} %fusion.63), channel_id=1, source_target_pairs={{0,126},{2,0},{4,2},{6,4},{8,6},{10,8},{12,10},{14,12},{16,14},{18... | collective-permute-start | bytes 776 | tf_op jit(solution)/shard_map/ppermute | solution.py:16
  101.3 1.3 collective-permute-start.5
  102.8 5.2 %collective-permute-done.5 = f32[2,1,10240]{2,1,0:T(1,128)S(1)} collective-permute-done((f32[2,1,10240]{2,1,0:T(1,128)S(1)}, f32[2,1,10240]{2,1,0:T(1,128)S(1)}, u32[]{:S(2)}, u32[]{:S(2)}) %collective-permute-start.5) | collective-permute-done | bytes 81952 | tf_op jit(solution)/shard_map/ppermute | solution.py:22
  108.6 0.9 fusion.56
  109.5 1.6 collective-permute-start.7
  111.4 3.4 %collective-permute-done.6 = f32[32,1]{1,0:T(8,128)S(1)} collective-permute-done((f32[32,1]{1,0:T(8,128)S(1)}, f32[32,1]{1,0:T(8,128)S(1)}, u32[]{:S(2)}, u32[]{:S(2)}) %collective-permute-start.6) | collective-permute-done | bytes 160 | tf_op jit(solution)/shard_map/ppermute | solution.py:16
  114.8 2.8 %subtract_bitcast_fusion = (f32[1,32,10240]{2,1,0:T(8,128)S(1)}, f32[32,10240]{1,0:T(8,128)S(1)}, f32[32,10240]{1,0:T(8,128)}) fusion(f32[32,10240]{1,0:T(8,128)S(1)} %get-tuple-element.15, f32[1,32,10240]{2,0,1:T(1,128)S(1)} %constant_dynamic-slice_fusion.1, f32[1,32,10240]{2,0,1:T(1,128)S(1)} %constant_dynamic-slice_fusion, f32[31,10240]{1,0:T(8,128)S(1)} %bitcast.156, ...), kind=kLoop, calls=%fused_computation.113 | loop fusion | flops 4587520 | bytes 13107200 | tf_op jit(solution)/shard_map/stack | solution.py:65
  118.4 6.8 %collective-permute-start.8 = (f32[2,32,1]{2,1,0:T(8,128)S(1)}, f32[2,32,1]{2,1,0:T(8,128)S(1)}, u32[]{:S(2)}, u32[]{:S(2)}) collective-permute-start(f32[2,32,1]{2,1,0:T(8,128)S(1)} %fusion.62), channel_id=1, source_target_pairs={{0,126},{2,0},{4,2},{6,4},{8,6},{10,8},{12,10},{14,12},{16,14},{18... | collective-permute-start | bytes 776 | tf_op jit(solution)/shard_map/ppermute | solution.py:16
  125.2 1.3 collective-permute-start.9
  126.7 5.9 %collective-permute-done.9 = f32[2,1,10240]{2,1,0:T(1,128)S(1)} collective-permute-done((f32[2,1,10240]{2,1,0:T(1,128)S(1)}, f32[2,1,10240]{2,1,0:T(1,128)S(1)}, u32[]{:S(2)}, u32[]{:S(2)}) %collective-permute-start.9) | collective-permute-done | bytes 81952 | tf_op jit(solution)/shard_map/ppermute | solution.py:22
  133.3 0.9 fusion.54
  134.3 1.6 collective-permute-start.11
  135.9 1.8 collective-permute-done.10
  137.7 5.6 %fusion.10 = (f32[]{:T(128)}, f32[]{:T(128)}, f32[]{:T(128)}, f32[32,10240]{1,0:T(8,128)S(1)}) fusion(f32[32,10240]{1,0:T(8,128)S(1)} %copy-done.11, f32[32,10240]{1,0:T(8,128)S(1)} %copy-done.3, f32[2,32,10240]{2,1,0:T(8,128)S(1)} %copy-done.7, f32[2,32,10240]{2,1,0:T(8,128)S(1)} %copy-done.9, f32[1,32,10240]{2,0,1:T(1,128)S(1)} %constant_dynamic-slice_fusion, ...), kind=kLoop, calls=%fused_computation.40 | loop fusion | flops 16711677 | bytes 23592972 | tf_op jit(solution)/shard_map/reduce_sum | solution.py:43
  143.3 2.1 add_divide_fusion
  145.4 68.2 %all-reduce = (f32[]{:T(128)}, f32[]{:T(128)}, f32[]{:T(128)}) all-reduce(f32[]{:T(128)} %get-tuple-element.5, f32[]{:T(128)} %get-tuple-element.6, f32[]{:T(128)} %get-tuple-element.4), channel_id=1, replica_groups=mesh['lon'=64,'lat'=2] {'lon','lat'}, use_global_device_ids=true, to_apply=%region_5.6 | all-reduce | flops 3 | bytes 24 | tf_op jit(solution)/shard_map/psum | solution.py:86
  (55 shorter events, 7.5 us)
Async XLA Ops:
  0.6 45.3 %all-to-all-start = ((f32[1,64,10240]{2,0,1:T(1,128)}), f32[1,64,10240]{2,0,1:T(1,128)S(1)}, u32[]{:S(2)}, u32[]{:S(2)}) async-start(f32[1,64,10240]{2,0,1:T(1,128)} %bitcast.161), calls=%async_computation | async-start | bytes 5242880 | tf_op jit(solution)/shard_map/all_to_all | solution.py:48
  46.0 1.6 copy-start.10
  47.5 45.6 %all-to-all-start.1 = ((f32[1,64,10240]{2,0,1:T(1,128)}), f32[1,64,10240]{2,0,1:T(1,128)}, u32[]{:S(2)}, u32[]{:S(2)}) async-start(f32[1,64,10240]{2,0,1:T(1,128)} %bitcast.162), calls=%async_computation.1 | async-start | bytes 5242880 | tf_op jit(solution)/shard_map/all_to_all | solution.py:49
  55.0 28.3 %collective-permute-start = (f32[2,32,1]{2,1,0:T(8,128)S(1)}, f32[2,32,1]{2,1,0:T(8,128)S(1)}, u32[]{:S(2)}, u32[]{:S(2)}) collective-permute-start(f32[2,32,1]{2,1,0:T(8,128)S(1)} %slice.145), channel_id=1, source_target_pairs={{0,126},{2,0},{4,2},{6,4},{8,6},{10,8},{12,10},{14,12},{16,14},{18... | collective-permute-start | bytes 776 | tf_op jit(solution)/shard_map/ppermute | solution.py:16
  55.4 30.2 %collective-permute-start.1 = (f32[2,1,10240]{2,1,0:T(1,128)S(1)}, f32[2,1,10240]{2,1,0:T(1,128)S(1)}, u32[]{:S(2)}, u32[]{:S(2)}) collective-permute-start(f32[2,1,10240]{2,1,0:T(1,128)S(1)} %slice.148), channel_id=1, source_target_pairs={{1,0},{3,2},{5,4},{7,6},{9,8},{11,10},{13,12},{15,14},{17,16},{19,... | collective-permute-start | bytes 245768 | tf_op jit(solution)/shard_map/ppermute | solution.py:22
  57.7 28.7 %copy-start.2 = (f32[32,10240]{1,0:T(8,128)S(1)}, f32[32,10240]{1,0:T(8,128)}, u32[]{:S(2)}) copy-start(f32[32,10240]{1,0:T(8,128)} %param.5) | copy-start | bytes 3932164
  86.3 1.6 copy-start.6
  86.3 2.3 %copy-start.8 = (f32[2,32,10240]{2,1,0:T(8,128)}, f32[2,32,10240]{2,1,0:T(8,128)S(1)}, u32[]{:S(2)}) copy-start(f32[2,32,10240]{2,1,0:T(8,128)S(1)} %get-tuple-element.28) | copy-start | bytes 7864324
  88.6 1.1 copy-start
  89.7 4.9 %collective-permute-start.2 = (f32[32,1]{1,0:T(8,128)S(1)}, f32[32,1]{1,0:T(8,128)S(1)}, u32[]{:S(2)}, u32[]{:S(2)}) collective-permute-start(f32[32,1]{1,0:T(8,128)S(1)} %slice.150), channel_id=1, source_target_pairs={{0,2},{2,4},{4,6},{6,8},{8,10},{10,12},{12,14},{14,16},{16,18},{18... | collective-permute-start | bytes 392 | tf_op jit(solution)/shard_map/ppermute | solution.py:16
  91.8 2.8 %collective-permute-start.3 = (f32[1,10240]{1,0:T(1,128)S(1)}, f32[1,10240]{1,0:T(1,128)S(1)}, u32[]{:S(2)}, u32[]{:S(2)}) collective-permute-start(f32[1,10240]{1,0:T(1,128)S(1)} %slice.152), channel_id=1, source_target_pairs={{0,1},{2,3},{4,5},{6,7},{8,9},{10,11},{12,13},{14,15},{16,17},{18,... | collective-permute-start | bytes 122888 | tf_op jit(solution)/shard_map/ppermute | solution.py:22
  93.1 1.7 copy-start.1
  98.3 4.5 %collective-permute-start.4 = (f32[2,32,1]{2,1,0:T(8,128)S(1)}, f32[2,32,1]{2,1,0:T(8,128)S(1)}, u32[]{:S(2)}, u32[]{:S(2)}) collective-permute-start(f32[2,32,1]{2,1,0:T(8,128)S(1)} %fusion.63), channel_id=1, source_target_pairs={{0,126},{2,0},{4,2},{6,4},{8,6},{10,8},{12,10},{14,12},{16,14},{18... | collective-permute-start | bytes 776 | tf_op jit(solution)/shard_map/ppermute | solution.py:16
  101.3 6.7 %collective-permute-start.5 = (f32[2,1,10240]{2,1,0:T(1,128)S(1)}, f32[2,1,10240]{2,1,0:T(1,128)S(1)}, u32[]{:S(2)}, u32[]{:S(2)}) collective-permute-start(f32[2,1,10240]{2,1,0:T(1,128)S(1)} %fusion.61), channel_id=1, source_target_pairs={{1,0},{3,2},{5,4},{7,6},{9,8},{11,10},{13,12},{15,14},{17,16},{19,... | collective-permute-start | bytes 245768 | tf_op jit(solution)/shard_map/ppermute | solution.py:22
  102.8 5.8 %copy-start.3 = (f32[32,10240]{1,0:T(8,128)S(1)}, f32[32,10240]{1,0:T(8,128)}, u32[]{:S(2)}) copy-start(f32[32,10240]{1,0:T(8,128)} %param.5) | copy-start | bytes 3932164
  109.5 5.3 %collective-permute-start.7 = (f32[1,10240]{1,0:T(1,128)S(1)}, f32[1,10240]{1,0:T(1,128)S(1)}, u32[]{:S(2)}, u32[]{:S(2)}) collective-permute-start(f32[1,10240]{1,0:T(1,128)S(1)} %slice.166), channel_id=1, source_target_pairs={{0,1},{2,3},{4,5},{6,7},{8,9},{10,11},{12,13},{14,15},{16,17},{18,... | collective-permute-start | bytes 122888 | tf_op jit(solution)/shard_map/ppermute | solution.py:22
  111.2 3.6 %collective-permute-start.6 = (f32[32,1]{1,0:T(8,128)S(1)}, f32[32,1]{1,0:T(8,128)S(1)}, u32[]{:S(2)}, u32[]{:S(2)}) collective-permute-start(f32[32,1]{1,0:T(8,128)S(1)} %slice.164), channel_id=1, source_target_pairs={{0,2},{2,4},{4,6},{6,8},{8,10},{10,12},{12,14},{14,16},{16,18},{18... | collective-permute-start | bytes 392 | tf_op jit(solution)/shard_map/ppermute | solution.py:16
  118.4 8.3 %collective-permute-start.8 = (f32[2,32,1]{2,1,0:T(8,128)S(1)}, f32[2,32,1]{2,1,0:T(8,128)S(1)}, u32[]{:S(2)}, u32[]{:S(2)}) collective-permute-start(f32[2,32,1]{2,1,0:T(8,128)S(1)} %fusion.62), channel_id=1, source_target_pairs={{0,126},{2,0},{4,2},{6,4},{8,6},{10,8},{12,10},{14,12},{16,14},{18... | collective-permute-start | bytes 776 | tf_op jit(solution)/shard_map/ppermute | solution.py:16
  125.2 7.4 %collective-permute-start.9 = (f32[2,1,10240]{2,1,0:T(1,128)S(1)}, f32[2,1,10240]{2,1,0:T(1,128)S(1)}, u32[]{:S(2)}, u32[]{:S(2)}) collective-permute-start(f32[2,1,10240]{2,1,0:T(1,128)S(1)} %fusion.60), channel_id=1, source_target_pairs={{1,0},{3,2},{5,4},{7,6},{9,8},{11,10},{13,12},{15,14},{17,16},{19,... | collective-permute-start | bytes 245768 | tf_op jit(solution)/shard_map/ppermute | solution.py:22
  133.3 4.4 %copy-start.7 = (f32[2,32,10240]{2,1,0:T(8,128)S(1)}, f32[2,32,10240]{2,1,0:T(8,128)}, u32[]{:S(2)}) copy-start(f32[2,32,10240]{2,1,0:T(8,128)} %copy-done.6) | copy-start | bytes 7864324
  133.3 4.4 %copy-start.9 = (f32[2,32,10240]{2,1,0:T(8,128)S(1)}, f32[2,32,10240]{2,1,0:T(8,128)}, u32[]{:S(2)}) copy-start(f32[2,32,10240]{2,1,0:T(8,128)} %copy-done.8) | copy-start | bytes 7864324
  133.3 4.4 %copy-start.11 = (f32[32,10240]{1,0:T(8,128)S(1)}, f32[32,10240]{1,0:T(8,128)}, u32[]{:S(2)}) copy-start(f32[32,10240]{1,0:T(8,128)} %get-tuple-element.16) | copy-start | bytes 3932164
  134.2 9.1 %copy-start.4 = (f32[32,10240]{1,0:T(8,128)}, f32[32,10240]{1,0:T(8,128)S(1)}, u32[]{:S(2)}) copy-start(f32[32,10240]{1,0:T(8,128)S(1)} %get-tuple-element.18) | copy-start | bytes 3932164
  134.2 9.1 %copy-start.5 = (f32[32,10240]{1,0:T(8,128)}, f32[32,10240]{1,0:T(8,128)S(1)}, u32[]{:S(2)}) copy-start(f32[32,10240]{1,0:T(8,128)S(1)} %get-tuple-element.17) | copy-start | bytes 3932164
  134.3 3.4 %collective-permute-start.11 = (f32[1,10240]{1,0:T(1,128)S(1)}, f32[1,10240]{1,0:T(1,128)S(1)}, u32[]{:S(2)}, u32[]{:S(2)}) collective-permute-start(f32[1,10240]{1,0:T(1,128)S(1)} %slice.180), channel_id=1, source_target_pairs={{0,1},{2,3},{4,5},{6,7},{8,9},{10,11},{12,13},{14,15},{16,17},{18,... | collective-permute-start | bytes 122888 | tf_op jit(solution)/shard_map/ppermute | solution.py:22
  135.9 1.8 collective-permute-start.10
where the time goes:
time: 217 us; the launch traced here: 216 us
  waiting for transfers between devices  79.2 us (36%)
  blocking collectives  68.2 us (31%)
  starting transfers between devices  36.2 us (17%)
  other arithmetic  20.2 us (9%)
  local copies, waits for them, and re-layouts  9.34 us (4%)
  between operations  2.9 us (1%)
    psum x1, blocking collectives, on_device(): gaps.append(lax.psum(local_gap, ('lon', 'lat')) / cells)  68.2 us
    all_to_all x1, waiting for transfers between devices, on_device(): lax.all_to_all(surface, 'lon', split_axis=1, concat_axis=0, tiled=True)  35 us
    ppermute x6, waiting for transfers between devices, shifted(): return lax.ppermute(value, axis, pairs)  30.8 us
    ppermute x6, waiting for transfers between devices, passed_along(): return lax.ppermute(block, axis, route)  13.5 us
    ppermute x6, starting transfers between devices, shifted(): return lax.ppermute(value, axis, pairs)  12.5 us
    all_to_all x1, starting transfers between devices, on_device(): lax.all_to_all(surface, 'lon', split_axis=1, concat_axis=0, tiled=True)  10.4 us
    ppermute x6, starting transfers between devices, passed_along(): return lax.ppermute(block, axis, route)  8.26 us
    another operation x10, other arithmetic, on_device(): stacked = jnp.stack([lead, heights])  7.46 us
  transfers between devices with their start and end apart: 14, of which 7 were waited for; matrix products, arithmetic and copies ran while one was open for 3% of the time, Pallas kernels for 0%

commit v1 on v0

v1 whole, which is shorter than its diff:
```python
import functools

import jax
import jax.numpy as jnp
from jax import lax
from jax.experimental import pallas as pl
from jax.experimental.pallas import tpu as pltpu
from jax.sharding import PartitionSpec as P

MESH = pl.DeviceIdType.MESH
STEP = 0.35
ITERS = 3
LANES = 128
ROWS = 32
CHUNKS = 80
LINE = 5120
WIN = 35
HALO = 15
PITCH = 112
CUTS = (0, 42, 66, 82)
PARTS = len(CUTS) - 1
FIRST, LAST = 1, 12


def kernel(
    surf_hbm, fid_hbm, smooth_hbm,
    out_h, out_x, out_y, gap_out,
    surf, fid, wgt, tile_in, height, dual_x, dual_y, slope_x, slope_y,
    acc, slots_a, slots_b,
    send_sem, recv_sem, relay_send, relay_recv, wrow_sem, wcol_sem, tile_sem, gap_send, gap_recv,
):
    lon = lax.axis_index("lon")
    lat = lax.axis_index("lat")
    core, x, zlo, y = lon % 2, (lon // 2) % 4, (lon // 8) % 2, lon // 16
    half = y // 2
    z_to = (zlo + lat + half) % 2
    own = lat == half
    slot = lon - 29 * half
    first = 3 * lat

    def lon_of(y_, zlo_, x_, core_):
        return ((y_ * 2 + zlo_) * 4 + x_) * 2 + core_

    tile_copy = pltpu.make_async_copy(smooth_hbm, tile_in, tile_sem)
    tile_copy.start()

    barrier = pltpu.get_barrier_semaphore()

    def greet(lon_, lat_):
        pl.semaphore_signal(barrier, inc=1, device_id=(lon_, lat_), device_id_type=MESH)

    def greet_source(k, carry):
        zs = (zlo + k) % 2
        zh = jnp.where(zs == zlo, lat, 1 - lat)
        src = lon_of(2 * lat + (k // 2) % 2, zs, (x + k // 8) % 4, (core + k // 4) % 2)

        @pl.when((src != lon) | (zh != lat))
        def _():
            greet(src, zh)

        return carry

    lax.fori_loop(0, 32, greet_source, 0)
    east, west = (lon + 1) % 64, (lon + 63) % 64
    greet(lon, 1 - lat)
    greet(east, lat)
    greet(west, lat)

    def peer_a(k):
        return lon_of(y, zlo, (x + k // 2) % 4, (core + k) % 2), lat

    def peer_b(k):
        return lon_of((y + k // 4) % 4, (zlo + k // 2) % 2, x, core), (lat + k) % 2

    def greet_a(k, carry):
        greet(*peer_a(k))
        return carry

    def greet_b(k, carry):
        greet(*peer_b(k))
        return carry

    lax.fori_loop(1, 8, greet_a, 0)
    lax.fori_loop(1, 16, greet_b, 0)

    tile_copy.wait()

    def lay(k, carry):
        blk, g = k // 10, k % 10
        for r8 in range(8):
            wgt[first + blk * 8 + r8, pl.ds(16 + 8 * g, 8), :] = tile_in[
                pl.ds(blk * 640 + g * 64 + r8, 8, stride=8), :
            ]
        return carry

    lax.fori_loop(0, 40, lay, 0)

    n_self = own.astype(jnp.int32)
    pl.semaphore_wait(barrier, 32 - n_self + 3 + 7 + 15)

    give = 29 - 26 * lat
    put = 32 * lat

    def row_copy(ref, lo, n, s_sem, r_sem):
        return pltpu.make_async_remote_copy(
            ref.at[pl.ds(give, 3), pl.ds(lo, n)],
            ref.at[pl.ds(put, 3), pl.ds(lo, n)],
            s_sem, r_sem, device_id=(lon, 1 - lat), device_id_type=MESH,
        )

    wrow = row_copy(wgt, HALO + 1, CHUNKS, wrow_sem.at[0], wrow_sem.at[1])
    wrow.start()

    def send_part(part):
        lo, hi = CUTS[part], CUTS[part + 1]

        def send(k, carry):
            dx = (k + 1) % 4
            dy = ((k % 16) // 4 + 4 - dx) % 4
            dst = lon_of((y + dy) % 4, z_to, (x + dx) % 4, (core + k // 16) % 2)
            here = (k == 3) & own

            def copy(i, a, b, at):
                src_ref = (surf_hbm, fid_hbm)[i].at[pl.ds(at, b - a)]
                dst_ref = (surf, fid)[i].at[slot, pl.ds(HALO + a, b - a)]

                @pl.when(here)
                def _():
                    pltpu.make_async_copy(src_ref, dst_ref, recv_sem.at[i, part]).start()

                @pl.when(jnp.logical_not(here))
                def _():
                    pltpu.make_async_remote_copy(
                        src_ref, dst_ref, send_sem.at[i], recv_sem.at[i, part],
                        device_id=(dst, half), device_id_type=MESH,
                    ).start()

            for i in range(2):
                start = dst * CHUNKS - 1
                if lo == 0:
                    @pl.when(dst == 0)
                    def _():
                        copy(i, 0, 1, LINE - 1)
                        copy(i, 1, hi, 0)

                    @pl.when(dst != 0)
                    def _():
                        copy(i, 0, hi, start)
                elif hi == CHUNKS + 2:
                    @pl.when(dst == 63)
                    def _():
                        copy(i, lo, hi - 1, LINE - CHUNKS - 1 + lo)
                        copy(i, hi - 1, hi, 0)

                    @pl.when(dst != 63)
                    def _():
                        copy(i, lo, hi, start + lo)
                else:
                    copy(i, lo, hi, start + lo)
            return carry

        lax.fori_loop(0, 32, send, 0)

    send_part(0)

    wrow.wait()
    wcols = [
        pltpu.make_async_remote_copy(
            wgt.at[pl.ds(0, WIN), pl.ds(at, 1)],
            wgt.at[pl.ds(0, WIN), pl.ds(to, 1)],
            wcol_sem.at[0, i], wcol_sem.at[1, i], device_id=(dev, lat), device_id_type=MESH,
        )
        for i, (at, to, dev) in enumerate(((HALO + CHUNKS, HALO, east), (HALO + 1, HALO + 1 + CHUNKS, west)))
    ]
    for c in wcols:
        c.start()
    for part in range(1, PARTS):
        send_part(part)

    lane = lax.broadcasted_iota(jnp.int32, (8, LANES), 1)
    is_first, is_last = lane == 0, lane == LANES - 1

    def at(ref, w, q):
        return ref[w, pl.ds(q, 8), :]

    def to_east(ref, w, q, mid):
        nxt = at(ref, w, q + 1)
        return pltpu.roll(jnp.where(is_first, nxt, mid), LANES - 1, 1)

    def to_west(ref, w, q, mid):
        prv = at(ref, w, q - 1)
        return pltpu.roll(jnp.where(is_last, prv, mid), 1, 1)

    def dual_row(step, w, q, mid, below):
        weight = at(wgt, w, q)
        ux = to_east(surf if step == 0 else height, w, q, mid) - mid
        uy = jnp.zeros_like(mid) if below is None else below - mid
        if step == 0:
            qx, qy = STEP * ux, STEP * uy
        else:
            qx = at(dual_x, w, q) + STEP * (2.0 * ux - at(slope_x, w, q))
            qy = at(dual_y, w, q) + STEP * (2.0 * uy - at(slope_y, w, q))
        if step < ITERS - 1:
            slope_x[w, pl.ds(q, 8), :] = ux
            slope_y[w, pl.ds(q, 8), :] = uy
        shrink = jnp.minimum(1.0, weight * lax.rsqrt(qx * qx + qy * qy))
        px, py = qx * shrink, qy * shrink
        dual_x[w, pl.ds(q, 8), :] = px
        dual_y[w, pl.ds(q, 8), :] = py
        return px, py, weight * jnp.sqrt(ux * ux + uy * uy)

    def primal_row(step, w, q, height_ref, py_north):
        px, py = at(dual_x, w, q), at(dual_y, w, q)
        d = px - to_west(dual_x, w, q, px) + py
        if py_north is not None:
            d = d - py_north
        h, s, f = at(height_ref, w, q), at(surf, w, q), at(fid, w, q)
        scaled = STEP * f
        damp = 1.0 + scaled
        both = 1.0 / (f * damp)
        term = d * (s + (0.5 * d) * (both * damp))
        if step > 0:
            miss = h - s
            term = term + (0.5 * f) * (miss * miss)
        new = (h + STEP * d + scaled * s) * (both * f)
        return py, new, term

    def masked(terms):
        low = jnp.where(lat == 0, terms[0] + terms[1] + terms[2], 0.0)
        top = jnp.where(lat == 1, terms[32] + terms[33] + terms[34], 0.0)
        return low + functools.reduce(jnp.add, terms[3:32]) + top

    def early(step, g0, g1):
        height_ref = surf if step == 0 else height

        def group(g, carry):
            q = pl.multiple_of(8 * g, 8)
            mid = at(height_ref, 0, q)
            terms = []
            for w in range(WIN):
                below = at(height_ref, w + 1, q) if w < WIN - 1 else None
                terms.append(dual_row(step, w, q, mid, below)[2])
                mid = below
            total = masked(terms)
            north = None
            terms = []
            for w in range(WIN):
                north, new, term = primal_row(step, w, q, height_ref, north)
                terms.append(term)
                height[w, pl.ds(q, 8), :] = new
            height[WIN, pl.ds(q, 8), :] = new
            in_tile = (g > FIRST) & (g < LAST)
            acc[step] += jnp.where(in_tile, total + masked(terms), 0.0)
            return carry

        if g1 > g0:
            lax.fori_loop(g0, g1, group, 0)

    def last_duals(q, place):
        mid = at(height, first, q)
        total = None
        for r in range(ROWS):
            w = first + r
            below = at(height, w + 1, q)
            px, py, term = dual_row(ITERS - 1, w, q, mid, below)
            if place is not None:
                out_x[place(r), :] = px
                out_y[place(r), :] = py
            total = term if total is None else total + term
            mid = below
        return total

    def last(g0, g1):
        def group(g, carry):
            q = pl.multiple_of(8 * g, 8)

            def place(r):
                return pl.ds(r // 8 * 640 + (g - FIRST - 1) * 64 + r % 8, 8, stride=8)

            w = jnp.where(lat == 0, WIN - 1, first - 1)
            north = dual_row(ITERS - 1, w, q, at(height, w, q), at(height, w + 1, q))[1]
            north = jnp.where(lat == 0, 0.0, north)
            total = last_duals(q, place)
            for r in range(ROWS):
                north, new, term = primal_row(ITERS - 1, first + r, q, height, north)
                out_h[place(r), :] = new
                total = total + term
            acc[ITERS - 1] += total
            return carry

        if g1 > g0:
            lax.fori_loop(g0, g1, group, 0)

    for step in range(ITERS):
        acc[step] = jnp.zeros((8, LANES), jnp.float32)

    done = FIRST
    for part in range(PARTS):
        lo, n = HALO + CUTS[part], CUTS[part + 1] - CUTS[part]
        for i, ref in enumerate((surf, fid)):
            got = ref.at[pl.ds(0, ROWS), pl.ds(lo, n)]
            pltpu.make_async_copy(got, got, recv_sem.at[i, part]).wait()
        relays = [
            row_copy(ref, lo, n, relay_send.at[i, part], relay_recv.at[i, part])
            for i, ref in enumerate((surf, fid))
        ]
        for c in relays:
            c.start()
        if part == 0:
            for c in wcols:
                c.wait()
        for c in relays:
            c.wait()

        final = part == PARTS - 1
        stop = LAST + 1 if final else (HALO + CUTS[part + 1] - 9) // 8 + 1
        early(0, done, stop)
        early(1, max(done - 1, FIRST), stop if final else stop - 1)
        if part == 0:
            last_duals(8 * FIRST, None)
        last(max(done - 2, FIRST + 1), stop - 1 if final else stop - 2)
        done = stop

    def total_of(ref, n):
        total = ref[0]
        for k in range(1, n):
            total = total + ref[k]
        return total

    rows = [jnp.sum(acc[step], axis=0, keepdims=True) for step in range(ITERS)]
    slots_a[0] = jnp.concatenate(rows + [jnp.zeros((5, LANES), jnp.float32)], axis=0)

    def spread(slots, n, peer, which):
        def go(k, carry):
            pltpu.make_async_remote_copy(
                slots.at[0], slots.at[k], gap_send.at[which], gap_recv.at[which],
                device_id=peer(k), device_id_type=MESH,
            ).start()
            return carry

        lax.fori_loop(1, n, go, 0)
        rest = slots.at[pl.ds(1, n - 1)]
        pltpu.make_async_copy(rest, rest, gap_recv.at[which]).wait()
        pltpu.make_async_copy(rest, rest, gap_send.at[which]).wait()

    spread(slots_a, 8, peer_a, 0)
    slots_b[0] = total_of(slots_a, 8)
    spread(slots_b, 16, peer_b, 1)
    gap_out[...] = jnp.sum(total_of(slots_b, 16), axis=1, keepdims=True) * (
        1.0 / (2 * ROWS * LINE * LANES)
    ) + jnp.zeros((8, LANES), jnp.float32)

    for i, ref in enumerate((surf, fid)):
        for n, cond in ((31, own), (32, jnp.logical_not(own))):
            @pl.when(cond)
            def _():
                sent = ref.at[pl.ds(0, n), pl.ds(0, CHUNKS + 2)]
                pltpu.make_async_copy(sent, sent, send_sem.at[i]).wait()


def on_device(surface, fidelity, smoothing):
    tile = smoothing.reshape(4, 8, CHUNKS, LANES).transpose(0, 2, 1, 3).reshape(-1, LANES)
    window = pltpu.VMEM((WIN + 1, PITCH, LANES), jnp.float32)
    flat = jax.ShapeDtypeStruct((ROWS * CHUNKS, LANES), jnp.float32)
    *outs, gap = pl.pallas_call(
        kernel,
        out_shape=[flat] * 3 + [jax.ShapeDtypeStruct((8, LANES), jnp.float32)],
        in_specs=[pl.BlockSpec(memory_space=pltpu.HBM)] * 3,
        out_specs=[pl.BlockSpec(memory_space=pltpu.VMEM)] * 4,
        scratch_shapes=[window] * 3
        + [pltpu.VMEM((ROWS * CHUNKS, LANES), jnp.float32)]
        + [window] * 5
        + [
            pltpu.VMEM((ITERS, 8, LANES), jnp.float32),
            pltpu.VMEM((8, 8, LANES), jnp.float32),
            pltpu.VMEM((16, 8, LANES), jnp.float32),
            pltpu.SemaphoreType.DMA((2,)),
            pltpu.SemaphoreType.DMA((2, PARTS)),
            pltpu.SemaphoreType.DMA((2, PARTS)),
            pltpu.SemaphoreType.DMA((2, PARTS)),
            pltpu.SemaphoreType.DMA((2,)),
            pltpu.SemaphoreType.DMA((2, 2)),
            pltpu.SemaphoreType.DMA,
            pltpu.SemaphoreType.DMA((2,)),
            pltpu.SemaphoreType.DMA((2,)),
        ],
        compiler_params=pltpu.CompilerParams(
            collective_id=0, has_side_effects=True, vmem_limit_bytes=48 * 2**20
        ),
    )(surface.reshape(LINE, LANES), fidelity.reshape(LINE, LANES), tile)
    tiles = [
        o.reshape(4, CHUNKS, 8, LANES).transpose(0, 2, 1, 3).reshape(ROWS, CHUNKS * LANES)
        for o in outs
    ]
    return (*tiles, gap[:ITERS, 0])


def solution(mesh):
    in_specs = (P("lon", None), P("lon", None), P("lat", "lon"))
    out_specs = (P("lat", "lon"), P("lat", "lon"), P("lat", "lon"), P())
    return jax.shard_map(
        on_device, mesh=mesh, in_specs=in_specs, out_specs=out_specs, check_vma=False
    )
```

time: 217 us -> 82.4 us (0.38)
  waiting for transfers between devices: 79.2 us -> 0 us
  Pallas kernels: 0 us -> 76.5 us
  blocking collectives: 68.2 us -> 0 us
  starting transfers between devices: 36.2 us -> 0 us
  other arithmetic: 20.2 us -> 0 us
  local copies, waits for them, and re-layouts: 9.34 us -> 5.1 us
  between operations: 2.9 us -> 0.65 us
    pallas_call x0 -> x1, Pallas kernels: none -> 76.5 us  [on_device(): pl.pallas_call(kernel, out_shape=[flat] * 3 + [jax.ShapeDtypeStruct((8, L...]
    psum x1 -> x0, blocking collectives: 68.2 us -> none  [on_device(): gaps.append(lax.psum(local_gap, ('lon', 'lat')) / cells)]
    ppermute x12 -> x0, waiting for transfers between devices: 44.3 us -> none  [the longest x6 30.8 us: shifted(): return lax.ppermute(value, axis, pairs)]
    all_to_all x2 -> x0, waiting for transfers between devices: 35 us -> none  [the longest x1 35 us: on_device(): lax.all_to_all(surface, 'lon', split_axis=1, concat_axis=0, tiled=True)]
    ppermute x12 -> x0, starting transfers between devices: 20.7 us -> none  [the longest x6 12.5 us: shifted(): return lax.ppermute(value, axis, pairs)]
    all_to_all x2 -> x0, starting transfers between devices: 15.5 us -> none  [the longest x1 10.4 us: on_device(): lax.all_to_all(surface, 'lon', split_axis=1, concat_axis=0, tiled=True)]
    another operation x11 -> x0, other arithmetic: 8.05 us -> none  [the longest x10 7.46 us: on_device(): stacked = jnp.stack([lead, heights])]
    reduce_sum x1 -> x0, other arithmetic: 5.57 us -> none  [advance(): return (updated, jnp.sum(terms))]
  transfers between devices with their start and end apart: 14 -> 0, of which waited for: 7 -> 0; matrix products, arithmetic and copies ran while one was open for 3% -> 0% of each run, Pallas kernels for 0% -> 0%
where the time goes in v1:
time: 82.4 us; the launch traced here: 82.3 us
  Pallas kernels  76.5 us (93%)
  local copies, waits for them, and re-layouts  5.1 us (6%)
    pallas_call x1, Pallas kernels, on_device(): pl.pallas_call(kernel, out_shape=[flat] * 3 + [jax.ShapeDtypeStruct((8, L...  76.5 us
    unnamed x5, local copies, waits for them, and re-layouts  4.48 us

profile of v1, /device:TPU:1, one launch (start us, length us, event | category | flops | bytes accessed | tf_op | source)
XLA Modules:
  0.0 82.3 jit_solution(5224552937098606826)
XLA Ops:
  0.6 0.0 copy-start
  0.6 1.3 %copy-done = f32[32,10240]{1,0:T(8,128)S(1)} copy-done((f32[32,10240]{1,0:T(8,128)S(1)}, f32[32,10240]{1,0:T(8,128)}, u32[]{:S(2)}) %copy-start) | copy-done | bytes 1310744
  1.9 76.5 %shard_map.66 = (f32[2560,128]{1,0:T(8,128)S(1)}, f32[2560,128]{1,0:T(8,128)S(1)}, f32[2560,128]{1,0:T(8,128)S(1)}, f32[8,128]{1,0:T(8,128)S(1)}) custom-call(f32[5120,128]{1,0:T(8,128)} %bitcast.26, f32[5120,128]{1,0:T(8,128)} %bitcast.27, f32[2560,128]{1,0:T(8,128)S(1)} %bitcast.25), custom_call_target="tpu_custom_call" | custom-call | tf_op jit(solution)/shard_map/pallas_call | solution.py:365
  78.5 0.6 slice_reduce_fusion
  79.1 1.1 %copy.10 = f32[32,10240]{1,0:T(8,128)} copy(f32[32,10240]{1,0:T(8,128)S(1)} %bitcast.24) | data formatting | bytes 2621440
  80.2 1.1 %copy.11 = f32[32,10240]{1,0:T(8,128)} copy(f32[32,10240]{1,0:T(8,128)S(1)} %bitcast.23) | data formatting | bytes 2621440
  81.2 1.1 %copy.12 = f32[32,10240]{1,0:T(8,128)} copy(f32[32,10240]{1,0:T(8,128)S(1)} %bitcast.22) | data formatting | bytes 2621440
Async XLA Ops:
  0.6 1.3 %copy-start = (f32[32,10240]{1,0:T(8,128)S(1)}, f32[32,10240]{1,0:T(8,128)}, u32[]{:S(2)}) copy-start(f32[32,10240]{1,0:T(8,128)} %param.5) | copy-start | bytes 3932164

commit v2 on v1

--- a/solution.py
+++ b/solution.py
@@ -98,17 +98,16 @@
     n_self = own.astype(jnp.int32)
     pl.semaphore_wait(barrier, 32 - n_self + 3 + 7 + 15)
 
-    give = 29 - 26 * lat
-    put = 32 * lat
-
-    def row_copy(ref, lo, n, s_sem, r_sem):
+    def row_copy(ref, depth, lo, n, s_sem, r_sem):
+        give = (32 - depth) * (1 - lat) + 3 * lat
+        put = (3 - depth) * (1 - lat) + 32 * lat
         return pltpu.make_async_remote_copy(
-            ref.at[pl.ds(give, 3), pl.ds(lo, n)],
-            ref.at[pl.ds(put, 3), pl.ds(lo, n)],
+            ref.at[pl.ds(give, depth), pl.ds(lo, n)],
+            ref.at[pl.ds(put, depth), pl.ds(lo, n)],
             s_sem, r_sem, device_id=(lon, 1 - lat), device_id_type=MESH,
         )
 
-    wrow = row_copy(wgt, HALO + 1, CHUNKS, wrow_sem.at[0], wrow_sem.at[1])
+    wrow = row_copy(wgt, 3, HALO + 1, CHUNKS, wrow_sem.at[0], wrow_sem.at[1])
     wrow.start()
 
     def send_part(part):
@@ -223,103 +222,126 @@
             miss = h - s
             term = term + (0.5 * f) * (miss * miss)
         new = (h + STEP * d + scaled * s) * (both * f)
-        return py, new, term
-
-    def masked(terms):
-        low = jnp.where(lat == 0, terms[0] + terms[1] + terms[2], 0.0)
-        top = jnp.where(lat == 1, terms[32] + terms[33] + terms[34], 0.0)
-        return low + functools.reduce(jnp.add, terms[3:32]) + top
-
-    def early(step, g0, g1):
-        height_ref = surf if step == 0 else height
-
-        def group(g, carry):
-            q = pl.multiple_of(8 * g, 8)
-            mid = at(height_ref, 0, q)
-            terms = []
-            for w in range(WIN):
-                below = at(height_ref, w + 1, q) if w < WIN - 1 else None
-                terms.append(dual_row(step, w, q, mid, below)[2])
-                mid = below
-            total = masked(terms)
-            north = None
-            terms = []
-            for w in range(WIN):
-                north, new, term = primal_row(step, w, q, height_ref, north)
-                terms.append(term)
+        return new, term
+
+    def count(step, g, terms):
+        def total(rows):
+            found = [terms[w] for w in rows if w in terms]
+            return functools.reduce(jnp.add, found) if found else None
+
+        parts = [total(range(3, 32))]
+        for rows, cond in ((range(3), lat == 0), (range(32, WIN), lat == 1)):
+            some = total(rows)
+            if some is not None:
+                parts.append(jnp.where(cond, some, 0.0))
+        some = functools.reduce(jnp.add, [p for p in parts if p is not None])
+        in_tile = (g > FIRST) & (g < LAST)
+        return jnp.where(in_tile, some, 0.0)
+
+    def place(w, g):
+        r = jnp.clip(w - first, 0, ROWS - 1)
+        return pl.ds(r // 8 * 640 + r % 8 + (g - FIRST - 1) * 64, 8, stride=8)
+
+    def duals(step, rows, g, write=True):
+        ref = surf if step == 0 else height
+        q = pl.multiple_of(8 * g, 8)
+        terms, seen = {}, {}
+
+        def row(w):
+            if w not in seen:
+                seen[w] = at(ref, w, q)
+            return seen[w]
+
+        for w in rows:
+            below = row(w + 1) if w < WIN - 1 else None
+            px, py, terms[w] = dual_row(step, w, q, row(w), below)
+            if step == ITERS - 1 and write:
+                out_x[place(w, g), :] = px
+                out_y[place(w, g), :] = py
+        return count(step, g, terms)
+
+    def primals(step, rows, g, write=True):
+        q = pl.multiple_of(8 * g, 8)
+        terms = {}
+        for w in rows:
+            north = at(dual_y, w - 1, q) if w > 0 else None
+            new, terms[w] = primal_row(step, w, q, surf if step == 0 else height, north)
+            if step < ITERS - 1:
                 height[w, pl.ds(q, 8), :] = new
-            height[WIN, pl.ds(q, 8), :] = new
-            in_tile = (g > FIRST) & (g < LAST)
-            acc[step] += jnp.where(in_tile, total + masked(terms), 0.0)
+            else:
+                out_h[place(w, g), :] = new
+        return count(step, g, terms)
+
+    def stage(fn, step, rows, g0, g1, write=True):
+        batch = max(1, 36 // len(rows))
+        whole = max(g1 - g0, 0) // batch
+
+        def body(g, n):
+            terms = [fn(step, rows, g + i, write) for i in range(n)]
+            acc[step] += functools.reduce(jnp.add, terms)
+
+        def go(k, carry):
+            body(g0 + k * batch, batch)
             return carry
 
-        if g1 > g0:
-            lax.fori_loop(g0, g1, group, 0)
-
-    def last_duals(q, place):
-        mid = at(height, first, q)
-        total = None
-        for r in range(ROWS):
-            w = first + r
-            below = at(height, w + 1, q)
-            px, py, term = dual_row(ITERS - 1, w, q, mid, below)
-            if place is not None:
-                out_x[place(r), :] = px
-                out_y[place(r), :] = py
-            total = term if total is None else total + term
-            mid = below
-        return total
-
-    def last(g0, g1):
-        def group(g, carry):
-            q = pl.multiple_of(8 * g, 8)
-
-            def place(r):
-                return pl.ds(r // 8 * 640 + (g - FIRST - 1) * 64 + r % 8, 8, stride=8)
-
-            w = jnp.where(lat == 0, WIN - 1, first - 1)
-            north = dual_row(ITERS - 1, w, q, at(height, w, q), at(height, w + 1, q))[1]
-            north = jnp.where(lat == 0, 0.0, north)
-            total = last_duals(q, place)
-            for r in range(ROWS):
-                north, new, term = primal_row(ITERS - 1, first + r, q, height, north)
-                out_h[place(r), :] = new
-                total = total + term
-            acc[ITERS - 1] += total
-            return carry
-
-        if g1 > g0:
-            lax.fori_loop(g0, g1, group, 0)
+        if whole:
+            lax.fori_loop(0, whole, go, 0)
+        if g0 + whole * batch < g1:
+            body(jnp.int32(g0 + whole * batch), g1 - g0 - whole * batch)
+
+    def sweep(inner, part):
+        done = FIRST if part == 0 else stop_of(part - 1)
+        stop = stop_of(part)
+        final = part == PARTS - 1
+
+        def rows(low, high):
+            if inner:
+                return list(range(low, high + 1))
+            return list(range(0, low)) + list(range(WIN - 1, high, -1))
+
+        for step in range(ITERS):
+            g0 = max(done - step, FIRST)
+            g1 = stop if final else stop - step
+            if step == ITERS - 1:
+                g1 = min(g1, LAST)
+                if g0 == FIRST:
+                    stage(duals, step, rows(3 + step, 30 - step), g0, g0 + 1, False)
+                    g0 += 1
+            stage(duals, step, rows(3 + step, 30 - step), g0, g1)
+            stage(primals, step, rows(4 + step, 30 - step), g0, g1)
+
+    def stop_of(part):
+        return LAST + 1 if part == PARTS - 1 else (HALO + CUTS[part + 1] - 9) // 8 + 1
 
     for step in range(ITERS):
         acc[step] = jnp.zeros((8, LANES), jnp.float32)
 
-    done = FIRST
+    def relays(part):
+        lo, n = HALO + CUTS[part], CUTS[part + 1] - CUTS[part]
+        return [
+            row_copy(ref, depth, lo, n, relay_send.at[i, part], relay_recv.at[i, part])
+            for i, (ref, depth) in enumerate(((surf, 3), (fid, 2)))
+        ]
+
+    def finish(part):
+        for c in relays(part):
+            c.wait()
+        sweep(False, part)
+
     for part in range(PARTS):
         lo, n = HALO + CUTS[part], CUTS[part + 1] - CUTS[part]
         for i, ref in enumerate((surf, fid)):
             got = ref.at[pl.ds(0, ROWS), pl.ds(lo, n)]
             pltpu.make_async_copy(got, got, recv_sem.at[i, part]).wait()
-        relays = [
-            row_copy(ref, lo, n, relay_send.at[i, part], relay_recv.at[i, part])
-            for i, ref in enumerate((surf, fid))
-        ]
-        for c in relays:
+        for c in relays(part):
             c.start()
         if part == 0:
             for c in wcols:
                 c.wait()
-        for c in relays:
-            c.wait()
-
-        final = part == PARTS - 1
-        stop = LAST + 1 if final else (HALO + CUTS[part + 1] - 9) // 8 + 1
-        early(0, done, stop)
-        early(1, max(done - 1, FIRST), stop if final else stop - 1)
-        if part == 0:
-            last_duals(8 * FIRST, None)
-        last(max(done - 2, FIRST + 1), stop - 1 if final else stop - 2)
-        done = stop
+        sweep(True, part)
+        if part > 0:
+            finish(part - 1)
+    finish(PARTS - 1)
 
     def total_of(ref, n):
         total = ref[0]
@@ -360,7 +382,7 @@
 
 def on_device(surface, fidelity, smoothing):
     tile = smoothing.reshape(4, 8, CHUNKS, LANES).transpose(0, 2, 1, 3).reshape(-1, LANES)
-    window = pltpu.VMEM((WIN + 1, PITCH, LANES), jnp.float32)
+    window = pltpu.VMEM((WIN, PITCH, LANES), jnp.float32)
     flat = jax.ShapeDtypeStruct((ROWS * CHUNKS, LANES), jnp.float32)
     *outs, gap = pl.pallas_call(
         kernel,

time: 82.4 us -> 72.3 us (0.88)
  Pallas kernels: 76.5 us -> 66.4 us
    pallas_call x1, Pallas kernels: 76.5 us -> 66.4 us  [on_device(): pl.pallas_call(kernel, out_shape=[flat] * 3 + [jax.ShapeDtypeStruct((8, L...]
where the time goes in v2:
time: 72.3 us; the launch traced here: 72.1 us
  Pallas kernels  66.4 us (92%)
  local copies, waits for them, and re-layouts  5.1 us (7%)
    pallas_call x1, Pallas kernels, on_device(): pl.pallas_call(kernel, out_shape=[flat] * 3 + [jax.ShapeDtypeStruct((8, L...  66.4 us
    unnamed x5, local copies, waits for them, and re-layouts  4.48 us

profile of v2, /device:TPU:1, one launch (start us, length us, event | category | flops | bytes accessed | tf_op | source)
XLA Modules:
  0.0 72.1 jit_solution(12470805362835238769)
XLA Ops:
  0.6 0.0 copy-start
  0.6 1.3 %copy-done = f32[32,10240]{1,0:T(8,128)S(1)} copy-done((f32[32,10240]{1,0:T(8,128)S(1)}, f32[32,10240]{1,0:T(8,128)}, u32[]{:S(2)}) %copy-start) | copy-done | bytes 1310744
  1.9 66.4 %shard_map.66 = (f32[2560,128]{1,0:T(8,128)S(1)}, f32[2560,128]{1,0:T(8,128)S(1)}, f32[2560,128]{1,0:T(8,128)S(1)}, f32[8,128]{1,0:T(8,128)S(1)}) custom-call(f32[5120,128]{1,0:T(8,128)} %bitcast.26, f32[5120,128]{1,0:T(8,128)} %bitcast.27, f32[2560,128]{1,0:T(8,128)S(1)} %bitcast.25), custom_call_target="tpu_custom_call" | custom-call | tf_op jit(solution)/shard_map/pallas_call | solution.py:387
  68.4 0.6 slice_reduce_fusion
  69.0 1.1 %copy.10 = f32[32,10240]{1,0:T(8,128)} copy(f32[32,10240]{1,0:T(8,128)S(1)} %bitcast.24) | data formatting | bytes 2621440
  70.0 1.1 %copy.11 = f32[32,10240]{1,0:T(8,128)} copy(f32[32,10240]{1,0:T(8,128)S(1)} %bitcast.23) | data formatting | bytes 2621440
  71.1 1.1 %copy.12 = f32[32,10240]{1,0:T(8,128)} copy(f32[32,10240]{1,0:T(8,128)S(1)} %bitcast.22) | data formatting | bytes 2621440
Async XLA Ops:
  0.6 1.3 %copy-start = (f32[32,10240]{1,0:T(8,128)S(1)}, f32[32,10240]{1,0:T(8,128)}, u32[]{:S(2)}) copy-start(f32[32,10240]{1,0:T(8,128)} %param.5) | copy-start | bytes 3932164

commit v3 on v2

--- a/solution.py
+++ b/solution.py
@@ -17,7 +17,7 @@
 WIN = 35
 HALO = 15
 PITCH = 112
-CUTS = (0, 42, 66, 82)
+CUTS = (0, 26, 50, 74, 82)
 PARTS = len(CUTS) - 1
 FIRST, LAST = 1, 12
 
@@ -27,7 +27,7 @@
     out_h, out_x, out_y, gap_out,
     surf, fid, wgt, tile_in, height, dual_x, dual_y, slope_x, slope_y,
     acc, slots_a, slots_b,
-    send_sem, recv_sem, relay_send, relay_recv, wrow_sem, wcol_sem, tile_sem, gap_send, gap_recv,
+    send_sem, recv_sem, relay_send, relay_recv, halo_sem, tile_sem, gap_send, gap_recv,
 ):
     lon = lax.axis_index("lon")
     lat = lax.axis_index("lat")
@@ -63,8 +63,9 @@
     lax.fori_loop(0, 32, greet_source, 0)
     east, west = (lon + 1) % 64, (lon + 63) % 64
     greet(lon, 1 - lat)
-    greet(east, lat)
-    greet(west, lat)
+    for lat_ in (lat, 1 - lat):
+        greet(east, lat_)
+        greet(west, lat_)
 
     def peer_a(k):
         return lon_of(y, zlo, (x + k // 2) % 4, (core + k) % 2), lat
@@ -96,7 +97,7 @@
     lax.fori_loop(0, 40, lay, 0)
 
     n_self = own.astype(jnp.int32)
-    pl.semaphore_wait(barrier, 32 - n_self + 3 + 7 + 15)
+    pl.semaphore_wait(barrier, 32 - n_self + 5 + 7 + 15)
 
     def row_copy(ref, depth, lo, n, s_sem, r_sem):
         give = (32 - depth) * (1 - lat) + 3 * lat
@@ -107,8 +108,31 @@
             s_sem, r_sem, device_id=(lon, 1 - lat), device_id_type=MESH,
         )
 
-    wrow = row_copy(wgt, 3, HALO + 1, CHUNKS, wrow_sem.at[0], wrow_sem.at[1])
-    wrow.start()
+    give_w, put_w = 29 * (1 - lat) + 3 * lat, 32 * lat
+    halo = [
+        pltpu.make_async_remote_copy(
+            wgt.at[pl.ds(give_w, 3), pl.ds(HALO + 1, CHUNKS)],
+            wgt.at[pl.ds(put_w, 3), pl.ds(HALO + 1, CHUNKS)],
+            halo_sem.at[0, 0], halo_sem.at[1, 0], device_id=(lon, 1 - lat), device_id_type=MESH,
+        )
+    ]
+    for i, (q0, q1, dev) in enumerate(
+        ((HALO + CHUNKS, HALO, east), (HALO + 1, HALO + 1 + CHUNKS, west))
+    ):
+        for j, (w0, w1, n, lat_) in enumerate(
+            ((first, first, ROWS, lat), (give_w, put_w, 3, 1 - lat))
+        ):
+            k = 1 + 2 * i + j
+            halo.append(
+                pltpu.make_async_remote_copy(
+                    wgt.at[pl.ds(w0, n), pl.ds(q0, 1)],
+                    wgt.at[pl.ds(w1, n), pl.ds(q1, 1)],
+                    halo_sem.at[0, k], halo_sem.at[1, k],
+                    device_id=(dev, lat_), device_id_type=MESH,
+                )
+            )
+    for c in halo:
+        c.start()
 
     def send_part(part):
         lo, hi = CUTS[part], CUTS[part + 1]
@@ -160,20 +184,7 @@
 
         lax.fori_loop(0, 32, send, 0)
 
-    send_part(0)
-
-    wrow.wait()
-    wcols = [
-        pltpu.make_async_remote_copy(
-            wgt.at[pl.ds(0, WIN), pl.ds(at, 1)],
-            wgt.at[pl.ds(0, WIN), pl.ds(to, 1)],
-            wcol_sem.at[0, i], wcol_sem.at[1, i], device_id=(dev, lat), device_id_type=MESH,
-        )
-        for i, (at, to, dev) in enumerate(((HALO + CHUNKS, HALO, east), (HALO + 1, HALO + 1 + CHUNKS, west)))
-    ]
-    for c in wcols:
-        c.start()
-    for part in range(1, PARTS):
+    for part in range(PARTS):
         send_part(part)
 
     lane = lax.broadcasted_iota(jnp.int32, (8, LANES), 1)
@@ -336,7 +347,7 @@
         for c in relays(part):
             c.start()
         if part == 0:
-            for c in wcols:
+            for c in halo:
                 c.wait()
         sweep(True, part)
         if part > 0:
@@ -400,8 +411,7 @@
             pltpu.SemaphoreType.DMA((2, PARTS)),
             pltpu.SemaphoreType.DMA((2, PARTS)),
             pltpu.SemaphoreType.DMA((2, PARTS)),
-            pltpu.SemaphoreType.DMA((2,)),
-            pltpu.SemaphoreType.DMA((2, 2)),
+            pltpu.SemaphoreType.DMA((2, 5)),
             pltpu.SemaphoreType.DMA,
             pltpu.SemaphoreType.DMA((2,)),
             pltpu.SemaphoreType.DMA((2,)),

time: 72.3 us -> 71 us (0.982)
  Pallas kernels: 66.4 us -> 65.1 us
    pallas_call x1, Pallas kernels: 66.4 us -> 65.1 us  [on_device(): pl.pallas_call(kernel, out_shape=[flat] * 3 + [jax.ShapeDtypeStruct((8, L...]
where the time goes in v3:
time: 71 us; the launch traced here: 70.8 us
  Pallas kernels  65.1 us (92%)
  local copies, waits for them, and re-layouts  5.1 us (7%)
    pallas_call x1, Pallas kernels, on_device(): pl.pallas_call(kernel, out_shape=[flat] * 3 + [jax.ShapeDtypeStruct((8, L...  65.1 us
    unnamed x5, local copies, waits for them, and re-layouts  4.48 us

profile of v3, /device:TPU:1, one launch (start us, length us, event | category | flops | bytes accessed | tf_op | source)
XLA Modules:
  0.0 70.8 jit_solution(10315951720965086461)
XLA Ops:
  0.6 0.0 copy-start
  0.6 1.3 %copy-done = f32[32,10240]{1,0:T(8,128)S(1)} copy-done((f32[32,10240]{1,0:T(8,128)S(1)}, f32[32,10240]{1,0:T(8,128)}, u32[]{:S(2)}) %copy-start) | copy-done | bytes 1310744
  1.9 65.1 %shard_map.66 = (f32[2560,128]{1,0:T(8,128)S(1)}, f32[2560,128]{1,0:T(8,128)S(1)}, f32[2560,128]{1,0:T(8,128)S(1)}, f32[8,128]{1,0:T(8,128)S(1)}) custom-call(f32[5120,128]{1,0:T(8,128)} %bitcast.26, f32[5120,128]{1,0:T(8,128)} %bitcast.27, f32[2560,128]{1,0:T(8,128)S(1)} %bitcast.25), custom_call_target="tpu_custom_call" | custom-call | tf_op jit(solution)/shard_map/pallas_call | solution.py:398
  67.0 0.6 slice_reduce_fusion
  67.7 1.1 %copy.10 = f32[32,10240]{1,0:T(8,128)} copy(f32[32,10240]{1,0:T(8,128)S(1)} %bitcast.24) | data formatting | bytes 2621440
  68.7 1.1 %copy.11 = f32[32,10240]{1,0:T(8,128)} copy(f32[32,10240]{1,0:T(8,128)S(1)} %bitcast.23) | data formatting | bytes 2621440
  69.8 1.1 %copy.12 = f32[32,10240]{1,0:T(8,128)} copy(f32[32,10240]{1,0:T(8,128)S(1)} %bitcast.22) | data formatting | bytes 2621440
Async XLA Ops:
  0.6 1.3 %copy-start = (f32[32,10240]{1,0:T(8,128)S(1)}, f32[32,10240]{1,0:T(8,128)}, u32[]{:S(2)}) copy-start(f32[32,10240]{1,0:T(8,128)} %param.5) | copy-start | bytes 3932164

commit v4 on v3

--- a/solution.py
+++ b/solution.py
@@ -51,7 +51,7 @@
 
     def greet_source(k, carry):
         zs = (zlo + k) % 2
-        zh = jnp.where(zs == zlo, lat, 1 - lat)
+        zh = jnp.where((zs == zlo) | (k < 8), lat, 1 - lat)
         src = lon_of(2 * lat + (k // 2) % 2, zs, (x + k // 8) % 4, (core + k // 4) % 2)
 
         @pl.when((src != lon) | (zh != lat))
@@ -96,8 +96,7 @@
 
     lax.fori_loop(0, 40, lay, 0)
 
-    n_self = own.astype(jnp.int32)
-    pl.semaphore_wait(barrier, 32 - n_self + 5 + 7 + 15)
+    pl.semaphore_wait(barrier, jnp.where(own, 39, 24) + 5 + 7 + 15)
 
     def row_copy(ref, depth, lo, n, s_sem, r_sem):
         give = (32 - depth) * (1 - lat) + 3 * lat
@@ -137,12 +136,21 @@
     def send_part(part):
         lo, hi = CUTS[part], CUTS[part + 1]
 
-        def send(k, carry):
+        def send(step, carry):
+            k, extra = step // 2, step % 2 == 1
             dx = (k + 1) % 4
             dy = ((k % 16) // 4 + 4 - dx) % 4
-            dst = lon_of((y + dy) % 4, z_to, (x + dx) % 4, (core + k // 16) % 2)
-            here = (k == 3) & own
-
+            z_dst = jnp.where(extra, 1 - zlo, z_to)
+            dst = lon_of((y + dy) % 4, z_dst, (x + dx) % 4, (core + k // 16) % 2)
+            here = (step == 6) & own
+
+            @pl.when(jnp.where(extra, own & (dx == 0), own | (dx != 0)))
+            def _():
+                send_block(dst, here)
+
+            return carry
+
+        def send_block(dst, here):
             def copy(i, a, b, at):
                 src_ref = (surf_hbm, fid_hbm)[i].at[pl.ds(at, b - a)]
                 dst_ref = (surf, fid)[i].at[slot, pl.ds(HALO + a, b - a)]
@@ -180,9 +188,8 @@
                         copy(i, lo, hi, start + lo)
                 else:
                     copy(i, lo, hi, start + lo)
-            return carry
-
-        lax.fori_loop(0, 32, send, 0)
+
+        lax.fori_loop(0, 64, send, 0)
 
     for part in range(PARTS):
         send_part(part)
@@ -327,16 +334,14 @@
     for step in range(ITERS):
         acc[step] = jnp.zeros((8, LANES), jnp.float32)
 
-    def relays(part):
+    def relay(part, i):
         lo, n = HALO + CUTS[part], CUTS[part + 1] - CUTS[part]
-        return [
-            row_copy(ref, depth, lo, n, relay_send.at[i, part], relay_recv.at[i, part])
-            for i, (ref, depth) in enumerate(((surf, 3), (fid, 2)))
-        ]
+        ref, depth = ((surf, 3), (fid, 2))[i]
+        return row_copy(ref, depth, lo, n, relay_send.at[i, part], relay_recv.at[i, part])
 
     def finish(part):
-        for c in relays(part):
-            c.wait()
+        for i in range(2):
+            relay(part, i).wait()
         sweep(False, part)
 
     for part in range(PARTS):
@@ -344,8 +349,7 @@
         for i, ref in enumerate((surf, fid)):
             got = ref.at[pl.ds(0, ROWS), pl.ds(lo, n)]
             pltpu.make_async_copy(got, got, recv_sem.at[i, part]).wait()
-        for c in relays(part):
-            c.start()
+            relay(part, i).start()
         if part == 0:
             for c in halo:
                 c.wait()
@@ -383,11 +387,11 @@
         1.0 / (2 * ROWS * LINE * LANES)
     ) + jnp.zeros((8, LANES), jnp.float32)
 
-    for i, ref in enumerate((surf, fid)):
-        for n, cond in ((31, own), (32, jnp.logical_not(own))):
+    for i, ref in enumerate((surf_hbm, fid_hbm)):
+        for n, cond in ((39, own), (24, jnp.logical_not(own))):
             @pl.when(cond)
             def _():
-                sent = ref.at[pl.ds(0, n), pl.ds(0, CHUNKS + 2)]
+                sent = ref.at[pl.ds(0, n * (CHUNKS + 2))]
                 pltpu.make_async_copy(sent, sent, send_sem.at[i]).wait()
 
 

time: 71 us -> 70.5 us (level)
  no operation moved by 1% of the time
where the time goes in v4:
time: 70.5 us; the launch traced here: 70.3 us
  Pallas kernels  64.6 us (92%)
  local copies, waits for them, and re-layouts  5.1 us (7%)
    pallas_call x1, Pallas kernels, on_device(): pl.pallas_call(kernel, out_shape=[flat] * 3 + [jax.ShapeDtypeStruct((8, L...  64.6 us
    unnamed x5, local copies, waits for them, and re-layouts  4.48 us

profile of v4, /device:TPU:1, one launch (start us, length us, event | category | flops | bytes accessed | tf_op | source)
XLA Modules:
  0.0 70.3 jit_solution(4815018917901027512)
XLA Ops:
  0.6 0.0 copy-start
  0.6 1.3 %copy-done = f32[32,10240]{1,0:T(8,128)S(1)} copy-done((f32[32,10240]{1,0:T(8,128)S(1)}, f32[32,10240]{1,0:T(8,128)}, u32[]{:S(2)}) %copy-start) | copy-done | bytes 1310744
  1.9 64.6 %shard_map.66 = (f32[2560,128]{1,0:T(8,128)S(1)}, f32[2560,128]{1,0:T(8,128)S(1)}, f32[2560,128]{1,0:T(8,128)S(1)}, f32[8,128]{1,0:T(8,128)S(1)}) custom-call(f32[5120,128]{1,0:T(8,128)} %bitcast.26, f32[5120,128]{1,0:T(8,128)} %bitcast.27, f32[2560,128]{1,0:T(8,128)S(1)} %bitcast.25), custom_call_target="tpu_custom_call" | custom-call | tf_op jit(solution)/shard_map/pallas_call | solution.py:402
  66.6 0.6 slice_reduce_fusion
  67.2 1.1 %copy.10 = f32[32,10240]{1,0:T(8,128)} copy(f32[32,10240]{1,0:T(8,128)S(1)} %bitcast.24) | data formatting | bytes 2621440
  68.2 1.1 %copy.11 = f32[32,10240]{1,0:T(8,128)} copy(f32[32,10240]{1,0:T(8,128)S(1)} %bitcast.23) | data formatting | bytes 2621440
  69.3 1.1 %copy.12 = f32[32,10240]{1,0:T(8,128)} copy(f32[32,10240]{1,0:T(8,128)S(1)} %bitcast.22) | data formatting | bytes 2621440
Async XLA Ops:
  0.6 1.3 %copy-start = (f32[32,10240]{1,0:T(8,128)S(1)}, f32[32,10240]{1,0:T(8,128)}, u32[]{:S(2)}) copy-start(f32[32,10240]{1,0:T(8,128)} %param.5) | copy-start | bytes 3932164
